TPU v7x, 128 devices: a whole 4x4x4 slice. The times are simulated.
128 devices in a mesh: src: 16 (over z_hi, x, core), snode: 8 (over y, z_lo).
Axes of the slice: x: 4, y: 4, z: 4 (z_hi: 2, z_lo: 2; z = z_hi * 2 + z_lo), core: 2. Of those that a mesh axis runs over, the one named last changes fastest.
Arguments:
- leaf_rhs: float32 [64, 256, 2048], P('snode', None, 'src'), may hold values from -6 to 6
- top_rhs: float32 [2048, 2048], P(None, 'src'), may hold values from -6 to 6
- leaf_inv: float32 [64, 256, 256], P('snode'), may hold values from -1 to 1, as said below
- coupling: float32 [64, 2048, 256], P('snode'), may hold values from -0.046875 to 0.046875
- top_inv: float32 [2048, 2048], P('snode'), may hold values from -1 to 1, as said below
- cond: float32 [64, 256], P('snode'), may hold values from 0.1 to 3
- electrodes: int32 [8192, 4], P('src'), may hold values from 0 to 2047, all different within a row
- blocks: int32 [16, 8192], P(None, 'src'), may hold values from 0 to 63
Outputs:
- sens: float32 [16, 256, 8192], P('snode', None, 'src')
Inputs may be any that keep to these rules, and one draw needn't show every extreme that they name: `electrodes`: the four sources of a row are different. `leaf_inv`: zero above the diagonal of each block. `top_inv`: zero above the diagonal.
All inputs are finite; a program needn't handle non-finite values.
Results may differ from a plain program's by a relative error of at most 0.00011.
Values sent between devices are 32-bit elements; how exact they have to be, the bound alone decides.
No kernel may reach another device: no remote copies, remote signals or barrier semaphores. Data moves between devices by JAX's collectives and lax.ppermute only.
A program may use at most 320 MiB of HBM per device.

v0:
```python
import jax
import jax.numpy as jnp
from jax import lax
from jax.sharding import PartitionSpec as P


def local(leaf_rhs, top_rhs, leaf_inv, coupling, top_inv, cond, electrodes, blocks):
    highest = lax.Precision.HIGHEST
    forward_leaf = jnp.einsum("bij,bjs->bis", leaf_inv, leaf_rhs, precision=highest)
    partial_value = jnp.einsum("bti,bis->ts", coupling, forward_leaf, precision=highest)
    coupled = lax.psum(partial_value, "snode")
    residual = top_rhs - coupled
    forward_top = jnp.dot(top_inv, residual, precision=highest)
    top_partial = jnp.einsum("rt,rs->ts", top_inv, forward_top, precision=highest)
    separator_field = lax.psum(top_partial, "snode")
    adjusted = forward_leaf - jnp.einsum(
        "bti,ts->bis", coupling, separator_field, precision=highest
    )
    leaf_field = jnp.einsum("bji,bjs->bis", leaf_inv, adjusted, precision=highest)
    leaves = leaf_field.shape[0]
    cells_n = leaf_field.shape[1]
    quads_n = electrodes.shape[0]
    shard_piece = lax.all_gather(leaf_field, "src", axis=2, tiled=True)
    width_n = shard_piece.shape[2]
    source_ids = lax.broadcasted_iota(jnp.int32, (width_n, quads_n), 0)

    def signed(plus_ids, minus_ids):
        upper = (source_ids == plus_ids[None, :]).astype(jnp.float32)
        lower = (source_ids == minus_ids[None, :]).astype(jnp.float32)
        return upper - lower

    current_sel = signed(electrodes[:, 0], electrodes[:, 1])
    potential_sel = signed(electrodes[:, 2], electrodes[:, 3])
    current_add = jnp.einsum("bcs,sq->bcq", shard_piece, current_sel, precision=highest)
    potential_add = jnp.einsum("bcs,sq->bcq", shard_piece, potential_sel, precision=highest)
    product = current_add * potential_add
    weighted = cond[:, :, None] * product
    owner_id = lax.axis_index("snode")
    local_blocks = blocks - owner_id * leaves
    own_rows = blocks.shape[0] // lax.axis_size("snode")
    summed = jnp.zeros((own_rows * lax.axis_size("snode"), cells_n, quads_n), jnp.float32)
    for leaf_id in range(leaves):
        summed = summed + jnp.where(
            (local_blocks == leaf_id)[:, None, :], weighted[leaf_id][None], 0.0
        )
    return lax.psum_scatter(summed, "snode", scatter_dimension=0, tiled=True)


def solution(mesh):
    return jax.shard_map(
        local,
        mesh=mesh,
        in_specs=(
            P("snode", None, "src"),
            P(None, "src"),
            P("snode", None, None),
            P("snode", None, None),
            P("snode", None),
            P("snode", None),
            P("src", None),
            P(None, "src"),
        ),
        out_specs=P("snode", None, "src"),
        check_vma=False,
    )
```

profile of v0, /device:TPU:1, one launch (start us, length us, event | category | flops | bytes accessed | tf_op | source)
XLA Modules:
  0.0 582.9 jit_solution(11139085248551137085)
XLA Ops:
  6.5 0.0 copy-start
  6.5 0.0 all-reduce.3.cloned.1.call-start
  6.5 1.6 copy-done
  8.1 3.2 fusion.21
  11.3 17.3 %convolution_bitcast_fusion = f32[2048,128]{1,0:T(8,128)} fusion(f32[8,256,128]{2,1,0:T(8,128)S(1)} %fusion.21, f32[8,2048,256]{2,1,0:T(8,128)} %param.11), kind=kOutput, calls=%fused_computation.16 | convolution fusion | flops 6442450944 | bytes 18874368 | tf_op jit(solution)/shard_map/bti,bis->ts/dot_general | solution.py:10
  28.6 0.0 all-reduce.3.cloned.1.call-update
  28.6 0.0 all-reduce.5.cloned.1.call-start
  28.6 76.9 %all-reduce.3.cloned.1.call-done = f32[2048,128]{1,0:T(8,128)} async-done(((f32[2048,128]{1,0:T(8,128)}), f32[2048,128]{1,0:T(8,128)}) %all-reduce.3.cloned.1.call-update) | async-done | bytes 1048592 | tf_op jit(solution)/shard_map/psum | solution.py:11
  105.5 0.0 copy-start.2
  105.6 4.2 fusion.18
  109.8 0.0 copy-done.2
  109.8 2.2 convolution_bitcast_fusion.1
  112.0 0.0 all-reduce.5.cloned.1.call-update
  112.0 0.3 all-gather.2.cloned.1.call-start
  112.3 77.3 %all-reduce.5.cloned.1.call-done = f32[2048,128]{0,1:T(8,128)} async-done(((f32[2048,128]{0,1:T(8,128)}), f32[2048,128]{0,1:T(8,128)}) %all-reduce.5.cloned.1.call-update) | async-done | bytes 1048592 | tf_op jit(solution)/shard_map/psum | solution.py:15
  189.6 29.2 %fusion.16 = f32[8,256,128]{2,1,0:T(8,128)S(1)} fusion(f32[8,256,128]{2,1,0:T(8,128)S(1)} %fusion.21, f32[8,2048,256]{2,1,0:T(8,128)} %param.11, f32[2048,128]{0,1:T(8,128)} %all-reduce.5.cloned.1.call-done), kind=kOutput, calls=%fused_computation.24 | convolution fusion | flops 6442713088 | bytes 19922944 | tf_op jit(solution)/shard_map/bti,ts->bis/dot_general | solution.py:16
  218.8 0.0 copy-start.4
  218.9 0.0 copy-start.3
  218.9 3.0 convolution_bitcast_fusion.2
  221.9 0.0 all-gather.2.cloned.1.call-update
  221.9 0.6 reduce-scatter.2.cloned.1.call-start
  222.5 0.0 copy-done.4
  222.5 0.0 copy-done.3
  222.6 113.9 %all-gather.2.cloned.1.call-done = f32[8,256,2048]{1,2,0:T(8,128)} async-done(((f32[8,256,128]{1,2,0:T(8,128)}), f32[8,256,2048]{1,2,0:T(8,128)}) %all-gather.2.cloned.1.call-update) | async-done | bytes 16777232 | tf_op jit(solution)/shard_map/all_gather | solution.py:23
  336.5 0.0 copy-start.5
  336.5 0.0 copy-start.6
  336.5 32.1 %fusion = f32[8,256,512]{2,1,0:T(8,128)S(1)} fusion(f32[8,256,2048]{1,2,0:T(8,128)} %all-gather.2.cloned.1.call-done, s32[512]{0:T(512)S(1)} %bitcast.57, s32[512]{0:T(512)S(1)} %bitcast.58), kind=kOutput, calls=%fused_computation.1 | convolution fusion | flops 25775046656 | bytes 20975616 | tf_op jit(solution)/shard_map/bcs,sq->bcq/dot_general | solution.py:35
  368.6 0.0 copy-done.5
  368.6 0.0 copy-done.6
  368.6 30.3 %multiply_multiply_fusion = f32[8,256,512]{2,1,0:T(8,128)S(1)} fusion(f32[8,256,512]{2,1,0:T(8,128)S(1)} %fusion, f32[8,256,2048]{1,2,0:T(8,128)S(1)} %copy-done.5, s32[512]{0:T(512)S(1)} %bitcast.56, s32[512]{0:T(512)S(1)} %bitcast.55, f32[8,256]{1,0:T(8,128)S(1)} %copy-done.6), kind=kOutput, calls=%fused_computation.5 | convolution fusion | flops 25777143808 | bytes 25178112 | tf_op jit(solution)/shard_map/bcs,sq->bcq/dot_general | solution.py:34
  398.9 0.5 slice_bitcast_fusion.7
  399.3 10.2 %select_add_fusion = f32[16,256,512]{2,1,0:T(8,128)} fusion(f32[256,512]{1,0:T(8,128)S(1)} %get-tuple-element.6, f32[256,512]{1,0:T(8,128)S(1)} %get-tuple-element.7, f32[256,512]{1,0:T(8,128)S(1)} %get-tuple-element.8, f32[256,512]{1,0:T(8,128)S(1)} %get-tuple-element.9, f32[256,512]{1,0:T(8,128)S(1)} %get-tuple-element.10, ...), kind=kLoop, calls=%fused_computation | loop fusion | flops 31457280 | bytes 12648448 | tf_op jit(solution)/shard_map/add | solution.py:43
  409.5 0.0 copy-start.1
  409.5 0.0 reduce-scatter.2.cloned.1.call-update
  409.5 166.6 %reduce-scatter.2.cloned.1.call-done = f32[2,256,512]{2,1,0:T(8,128)} async-done(((f32[16,256,512]{2,1,0:T(8,128)}), f32[2,256,512]{2,1,0:T(8,128)}) %reduce-scatter.2.cloned.1.call-update) | async-done | bytes 1048592 | tf_op jit(solution)/shard_map/reduce_scatter | solution.py:46
  576.1 0.0 copy-done.1
  (2 shorter events, 0.1 us)
Async XLA Ops:
  6.5 1.6 copy-start
  6.5 99.0 %all-reduce.3.cloned.1.call-start = ((), (), s32[]{:S(2)}) async-start(), calls=%async_computation.1 | async-start | bytes 2097152 | tf_op jit(solution)/shard_map/psum | solution.py:11
  28.6 161.1 %all-reduce.5.cloned.1.call-start = ((), (), s32[]{:S(2)}) async-start(), calls=%async_computation.2 | async-start | bytes 2097152 | tf_op jit(solution)/shard_map/psum | solution.py:15
  105.5 4.2 copy-start.2
  112.0 224.5 %all-gather.2.cloned.1.call-start = ((), (), s32[]{:S(2)}) async-start(), calls=%async_computation.3 | async-start | bytes 17825792 | tf_op jit(solution)/shard_map/all_gather | solution.py:23
  218.8 3.6 copy-start.4
  218.9 3.6 copy-start.3
  221.9 354.2 %reduce-scatter.2.cloned.1.call-start = ((), (), s32[]{:S(2)}) async-start(), calls=%async_computation.4 | async-start | bytes 9437184 | tf_op jit(solution)/shard_map/reduce_scatter | solution.py:46
  336.5 32.1 %copy-start.5 = (f32[8,256,2048]{1,2,0:T(8,128)S(1)}, f32[8,256,2048]{1,2,0:T(8,128)}, u32[]{:S(2)}) copy-start(f32[8,256,2048]{1,2,0:T(8,128)} %all-gather.2.cloned.1.call-done) | copy-start | bytes 50331652
  336.5 32.1 %copy-start.6 = (f32[8,256]{1,0:T(8,128)S(1)}, f32[8,256]{1,0:T(8,128)}, u32[]{:S(2)}) copy-start(f32[8,256]{1,0:T(8,128)} %param.13) | copy-start | bytes 24580
  409.5 166.6 %copy-start.1 = (f32[8,256,256]{2,1,0:T(8,128)S(1)}, f32[8,256,256]{2,1,0:T(8,128)}, u32[]{:S(2)}) copy-start(f32[8,256,256]{2,1,0:T(8,128)} %param.10) | copy-start | bytes 6291460
Sparse Core Ops, SparseCore 0:
  28.7 76.7 all-reduce.2
  112.1 77.4 all-reduce.4
  222.0 114.4 all-gather.1
  409.7 166.3 reduce-scatter.1
where the time goes:
time: 590 us; the launch traced here: 583 us
  waiting for transfers between devices  435 us (74%)
  matrix products  121 us (21%)
  between operations  13.5 us (2%)
  other arithmetic  10.2 us (2%)
    reduce_scatter x1, waiting for transfers between devices, local(): return lax.psum_scatter(summed, 'snode', scatter_dimension=0, tiled=True)  167 us
    all_gather x1, waiting for transfers between devices, local(): shard_piece = lax.all_gather(leaf_field, 'src', axis=2, tiled=True)  114 us
    psum x1, waiting for transfers between devices, local(): separator_field = lax.psum(top_partial, 'snode')  77.3 us
    psum x1, waiting for transfers between devices, local(): coupled = lax.psum(partial_value, 'snode')  76.9 us
    dot_general x1, matrix products, local(): jnp.einsum('bcs,sq->bcq', shard_piece, potential_sel, precision=highest)  32.1 us
    dot_general x1, matrix products, local(): jnp.einsum('bcs,sq->bcq', shard_piece, current_sel, precision=highest)  30.3 us
    dot_general x1, matrix products, local(): jnp.einsum('bti,ts->bis', coupling, separator_field, precision=highest)  29.2 us
    dot_general x1, matrix products, local(): jnp.einsum('bti,bis->ts', coupling, forward_leaf, precision=highest)  17.3 us
  transfers between devices with their start and end apart: 4, of which 4 were waited for; matrix products, arithmetic and copies ran while one was open for 0% of the time, Pallas kernels for 0%

commit v1 on v0

--- a/solution.py
+++ b/solution.py
@@ -8,7 +8,7 @@
     highest = lax.Precision.HIGHEST
     forward_leaf = jnp.einsum("bij,bjs->bis", leaf_inv, leaf_rhs, precision=highest)
     partial_value = jnp.einsum("bti,bis->ts", coupling, forward_leaf, precision=highest)
-    coupled = lax.psum(partial_value, "snode")
+    coupled = jnp.sum(lax.all_gather(partial_value, "snode"), axis=0)
     residual = top_rhs - coupled
     forward_top = jnp.dot(top_inv, residual, precision=highest)
     top_partial = jnp.einsum("rt,rs->ts", top_inv, forward_top, precision=highest)

time: 590 us -> 698 us (1.18)
  waiting for transfers between devices: 435 us -> 529 us
  local copies, waits for them, and re-layouts: 2.08 us -> 14.5 us
    all_gather x0 -> x1, waiting for transfers between devices: none -> 169 us  [local(): coupled = jnp.sum(lax.all_gather(partial_value, 'snode'), axis=0)]
    psum x1 -> x0, waiting for transfers between devices: 76.9 us -> none  [local(): coupled = lax.psum(partial_value, 'snode')]
    unnamed x14 -> x18, local copies, waits for them, and re-layouts: 1.62 us -> 14 us
where the time goes in v1:
time: 698 us; the launch traced here: 694 us
  waiting for transfers between devices  529 us (76%)
  matrix products  124 us (18%)
  local copies, waits for them, and re-layouts  14.5 us (2%)
  between operations  13.6 us (2%)
  other arithmetic  12.3 us (2%)
    all_gather x1, waiting for transfers between devices, local(): coupled = jnp.sum(lax.all_gather(partial_value, 'snode'), axis=0)  169 us
    reduce_scatter x1, waiting for transfers between devices, local(): return lax.psum_scatter(summed, 'snode', scatter_dimension=0, tiled=True)  167 us
    all_gather x1, waiting for transfers between devices, local(): shard_piece = lax.all_gather(leaf_field, 'src', axis=2, tiled=True)  114 us
    psum x1, waiting for transfers between devices, local(): separator_field = lax.psum(top_partial, 'snode')  79.2 us
    dot_general x1, matrix products, local(): jnp.einsum('bcs,sq->bcq', shard_piece, potential_sel, precision=highest)  32.1 us
    dot_general x1, matrix products, local(): jnp.einsum('bcs,sq->bcq', shard_piece, current_sel, precision=highest)  30.4 us
    dot_general x1, matrix products, local(): jnp.einsum('bti,ts->bis', coupling, separator_field, precision=highest)  29.2 us
    dot_general x1, matrix products, local(): jnp.einsum('bti,bis->ts', coupling, forward_leaf, precision=highest)  21.2 us
  transfers between devices with their start and end apart: 4, of which 4 were waited for; matrix products, arithmetic and copies ran while one was open for 0% of the time, Pallas kernels for 0%

profile of v1, /device:TPU:1, one launch (start us, length us, event | category | flops | bytes accessed | tf_op | source)
XLA Modules:
  0.0 693.6 jit_solution(3814288037586335014)
XLA Ops:
  6.5 0.0 copy-start
  6.5 0.0 all-gather.6.cloned.1.call-start
  6.5 1.6 copy-done
  8.1 3.2 fusion.21
  11.3 21.2 %convolution_bitcast_fusion = f32[2048,128]{0,1:T(8,128)} fusion(f32[8,256,128]{2,1,0:T(8,128)S(1)} %fusion.21, f32[8,2048,256]{2,1,0:T(8,128)} %param.11), kind=kOutput, calls=%fused_computation.17 | convolution fusion | flops 6442450944 | bytes 18874368 | tf_op jit(solution)/shard_map/bti,bis->ts/dot_general | solution.py:10
  32.5 0.0 all-gather.6.cloned.1.call-update
  32.6 0.6 all-reduce.2.cloned.1.call-start
  33.1 2.5 copy.14
  35.7 168.7 %all-gather.6.cloned.1.call-done = f32[16384,128]{0,1:T(8,128)} async-done(((f32[2048,128]{0,1:T(8,128)}), f32[16384,128]{0,1:T(8,128)}) %all-gather.6.cloned.1.call-update) | async-done | bytes 8388624 | tf_op jit(solution)/shard_map/all_gather | solution.py:11
  204.3 9.9 %copy.22 = f32[16,8,8,2048]{3,2,1,0:T(8,128)S(1)} copy(f32[16,8,8,2048]{3,1,2,0:T(8,128)} %bitcast.60) | data formatting | bytes 16777216
  214.2 0.0 copy-start.2
  214.2 0.0 copy-start.3
  214.2 2.0 bitcast_reduce_fusion
  216.2 0.0 copy-done.2
  216.2 0.0 copy-done.3
  216.2 2.2 fusion.18
  218.5 2.4 convolution_bitcast_fusion.1
  220.9 0.0 all-reduce.2.cloned.1.call-update
  220.9 0.0 all-gather.4.cloned.1.call-start
  220.9 79.2 %all-reduce.2.cloned.1.call-done = f32[2048,128]{0,1:T(8,128)} async-done(((f32[2048,128]{0,1:T(8,128)}), f32[2048,128]{0,1:T(8,128)}) %all-reduce.2.cloned.1.call-update) | async-done | bytes 1048592 | tf_op jit(solution)/shard_map/psum | solution.py:15
  300.1 29.2 %fusion.16 = f32[8,256,128]{2,1,0:T(8,128)S(1)} fusion(f32[8,256,128]{2,1,0:T(8,128)S(1)} %fusion.21, f32[8,2048,256]{2,1,0:T(8,128)} %param.11, f32[2048,128]{0,1:T(8,128)} %all-reduce.2.cloned.1.call-done), kind=kOutput, calls=%fused_computation.25 | convolution fusion | flops 6442713088 | bytes 19922944 | tf_op jit(solution)/shard_map/bti,ts->bis/dot_general | solution.py:16
  329.3 0.0 copy-start.5
  329.3 0.0 copy-start.4
  329.3 3.0 convolution_bitcast_fusion.2
  332.3 0.0 all-gather.4.cloned.1.call-update
  332.3 0.3 reduce-scatter.2.cloned.1.call-start
  332.6 0.0 copy-done.5
  332.6 0.0 copy-done.4
  332.7 114.2 %all-gather.4.cloned.1.call-done = f32[8,256,2048]{1,2,0:T(8,128)} async-done(((f32[8,256,128]{1,2,0:T(8,128)}), f32[8,256,2048]{1,2,0:T(8,128)}) %all-gather.4.cloned.1.call-update) | async-done | bytes 16777232 | tf_op jit(solution)/shard_map/all_gather | solution.py:23
  446.9 0.0 copy-start.6
  446.9 0.0 copy-start.7
  446.9 32.1 %fusion = f32[8,256,512]{2,1,0:T(8,128)S(1)} fusion(f32[8,256,2048]{1,2,0:T(8,128)} %all-gather.4.cloned.1.call-done, s32[512]{0:T(512)S(1)} %bitcast.63, s32[512]{0:T(512)S(1)} %bitcast.64), kind=kOutput, calls=%fused_computation.2 | convolution fusion | flops 25775046656 | bytes 20975616 | tf_op jit(solution)/shard_map/bcs,sq->bcq/dot_general | solution.py:35
  479.0 0.0 copy-done.6
  479.0 0.0 copy-done.7
  479.0 30.4 %multiply_multiply_fusion = f32[8,256,512]{2,1,0:T(8,128)S(1)} fusion(f32[8,256,512]{2,1,0:T(8,128)S(1)} %fusion, f32[8,256,2048]{1,2,0:T(8,128)S(1)} %copy-done.6, s32[512]{0:T(512)S(1)} %bitcast.62, s32[512]{0:T(512)S(1)} %bitcast.61, f32[8,256]{1,0:T(8,128)S(1)} %copy-done.7), kind=kOutput, calls=%fused_computation.6 | convolution fusion | flops 25777143808 | bytes 25178112 | tf_op jit(solution)/shard_map/bcs,sq->bcq/dot_general | solution.py:34
  509.4 0.5 slice_bitcast_fusion.7
  509.9 10.3 %select_add_fusion = f32[16,256,512]{2,1,0:T(8,128)} fusion(f32[256,512]{1,0:T(8,128)S(1)} %get-tuple-element.6, f32[256,512]{1,0:T(8,128)S(1)} %get-tuple-element.7, f32[256,512]{1,0:T(8,128)S(1)} %get-tuple-element.8, f32[256,512]{1,0:T(8,128)S(1)} %get-tuple-element.9, f32[256,512]{1,0:T(8,128)S(1)} %get-tuple-element.10, ...), kind=kLoop, calls=%fused_computation.1 | loop fusion | flops 31457280 | bytes 12648448 | tf_op jit(solution)/shard_map/add | solution.py:43
  520.1 0.0 copy-start.1
  520.1 0.0 reduce-scatter.2.cloned.1.call-update
  520.1 166.6 %reduce-scatter.2.cloned.1.call-done = f32[2,256,512]{2,1,0:T(8,128)} async-done(((f32[16,256,512]{2,1,0:T(8,128)}), f32[2,256,512]{2,1,0:T(8,128)}) %reduce-scatter.2.cloned.1.call-update) | async-done | bytes 1048592 | tf_op jit(solution)/shard_map/reduce_scatter | solution.py:46
  686.7 0.0 copy-done.1
  (2 shorter events, 0.1 us)
Async XLA Ops:
  6.5 1.6 copy-start
  6.5 197.8 %all-gather.6.cloned.1.call-start = ((), (), s32[]{:S(2)}) async-start(), calls=%async_computation.4 | async-start | bytes 9437184 | tf_op jit(solution)/shard_map/all_gather | solution.py:11
  32.6 267.5 %all-reduce.2.cloned.1.call-start = ((), (), s32[]{:S(2)}) async-start(), calls=%async_computation.1 | async-start | bytes 2097152 | tf_op jit(solution)/shard_map/psum | solution.py:15
  214.2 2.0 copy-start.2
  214.2 2.0 copy-start.3
  220.9 226.0 %all-gather.4.cloned.1.call-start = ((), (), s32[]{:S(2)}) async-start(), calls=%async_computation.2 | async-start | bytes 17825792 | tf_op jit(solution)/shard_map/all_gather | solution.py:23
  329.3 3.3 copy-start.5
  329.3 3.3 copy-start.4
  332.3 354.4 %reduce-scatter.2.cloned.1.call-start = ((), (), s32[]{:S(2)}) async-start(), calls=%async_computation.3 | async-start | bytes 9437184 | tf_op jit(solution)/shard_map/reduce_scatter | solution.py:46
  446.9 32.1 %copy-start.6 = (f32[8,256,2048]{1,2,0:T(8,128)S(1)}, f32[8,256,2048]{1,2,0:T(8,128)}, u32[]{:S(2)}) copy-start(f32[8,256,2048]{1,2,0:T(8,128)} %all-gather.4.cloned.1.call-done) | copy-start | bytes 50331652
  446.9 32.1 %copy-start.7 = (f32[8,256]{1,0:T(8,128)S(1)}, f32[8,256]{1,0:T(8,128)}, u32[]{:S(2)}) copy-start(f32[8,256]{1,0:T(8,128)} %param.13) | copy-start | bytes 24580
  520.1 166.6 %copy-start.1 = (f32[8,256,256]{2,1,0:T(8,128)S(1)}, f32[8,256,256]{2,1,0:T(8,128)}, u32[]{:S(2)}) copy-start(f32[8,256,256]{2,1,0:T(8,128)} %param.10) | copy-start | bytes 6291460
Sparse Core Ops, SparseCore 0:
  32.7 171.5 all-gather.5
  221.0 79.0 all-reduce.1
  332.5 114.4 all-gather.3
  520.3 166.3 reduce-scatter.1
